TPU v7x, 32 devices: a whole 2x2x4 slice. The times are simulated.
32 devices in a mesh: groups: 2 (over x), lon: 16 (over z, y, core).
Axes of the slice: x: 2, y: 2, z: 4, core: 2. Of those that a mesh axis runs over, the one named last changes fastest.
Arguments:
- flux_probes: bfloat16 [768, 8, 192, 256], P('lon', 'groups'), parts along dimension 1, may hold values from -6 to 6
- time_factor: bfloat16 [192, 192], replicated, as said below
- lat_factor: bfloat16 [256, 256], replicated, as said below
- lon_factor: bfloat16 [768, 768], replicated, as said below
- footprint: bfloat16 [1024, 128, 128], P('lon'), may hold values from -0.5 to 0.5
- entry_owner: int32 [1024, 1], P('lon'), may hold values from 0 to 15; in each aligned block of 64 rows (0 to 63, 64 to 127, ...) at most 8 rows name the same one
- entry_block: int32 [1024], P('lon'), may hold values from 0 to 7
- entry_tile: int32 [1024], P('lon'), may hold values from 0 to 18431
- obs_weight: float32 [128, 128], P('lon'), may hold values from 0.1 to 1
Outputs:
- hessian_probes: bfloat16 [768, 8, 192, 256], P('lon', 'groups'), parts along dimension 1
There are 2 independent parts, one for each index of `groups`. A program takes and returns all parts, laid end to end along the dimension named above; an argument that names none is the same for every part. Nothing has to cross between parts.
Inputs may be any that keep to these rules, and one draw needn't show every extreme that they name: `entry_owner`: on each device at most 8 of its 64 footprint tiles belong to one owner, and some owner has exactly 8. `time_factor`: lower triangular with a positive diagonal. `lat_factor`: lower triangular with a positive diagonal. `lon_factor`: lower triangular with a positive diagonal.
All inputs are finite; a program needn't handle non-finite values.
Results may differ from a plain program's by a relative error of at most 0.0034.
Values may be sent and summed in bfloat16 or wider, within the bound.
A program may use at most 192 MiB of HBM per device.

v0:
```python
import jax
import jax.numpy as jnp
from jax import lax
from jax.sharding import PartitionSpec as P

SND = 128


def body(
    flux_probes,
    time_factor,
    lat_factor,
    lon_factor,
    footprint,
    entry_owner,
    entry_block,
    entry_tile,
    obs_weight,
):
    f32 = jnp.float32
    devices = lax.axis_size("lon")
    lon_dev, probe_count, days, lats = flux_probes.shape
    longitudes = lon_factor.shape[0]
    bands = lats // SND
    day_dev = days // devices
    blocks_dev = obs_weight.shape[0]
    lat_mixed = jnp.einsum(
        "optj,ij->opti", flux_probes, lat_factor, preferred_element_type=f32
    ).astype(jnp.bfloat16)
    time_mixed = jnp.einsum(
        "ts,opsi->opti", time_factor, lat_mixed, preferred_element_type=f32
    ).astype(jnp.bfloat16)
    day_slab = lax.all_to_all(time_mixed, "lon", split_axis=2, concat_axis=0, tiled=True)
    prior_field = jnp.einsum(
        "ko,optl->kptl", lon_factor, day_slab, preferred_element_type=f32
    ).astype(jnp.bfloat16)
    lon_idx = entry_tile // (day_dev * bands)
    day_idx = entry_tile // bands % day_dev
    band_idx = entry_tile % bands
    shaped = prior_field.reshape(longitudes, probe_count, day_dev, bands, SND)
    tile_values = shaped[lon_idx, :, day_idx, band_idx, :]
    partial_value = jnp.einsum("erc,epc->epr", footprint, tile_values, preferred_element_type=f32)
    owners = entry_owner[:, 0]
    global_block = owners * blocks_dev + entry_block
    dense_sums = (
        jnp.zeros((devices * blocks_dev, probe_count, SND), f32).at[global_block].add(partial_value)
    )
    modeled = lax.psum_scatter(dense_sums, "lon", scatter_dimension=0, tiled=True)
    weighted = (obs_weight[:, None, :] * modeled).astype(jnp.bfloat16)
    all_weighted = lax.all_gather(weighted, "lon", axis=0, tiled=True)
    entry_resid = all_weighted[global_block]
    back_tile = jnp.einsum("erc,epr->epc", footprint, entry_resid, preferred_element_type=f32)
    adjoint = (
        jnp.zeros((longitudes, probe_count, day_dev, bands, SND), f32)
        .at[lon_idx, :, day_idx, band_idx, :]
        .add(back_tile)
    )
    adjoint_field = adjoint.reshape(longitudes, probe_count, day_dev, lats).astype(jnp.bfloat16)
    lon_back = jnp.einsum(
        "ko,kptl->optl", lon_factor, adjoint_field, preferred_element_type=f32
    ).astype(jnp.bfloat16)
    band_slab = lax.all_to_all(lon_back, "lon", split_axis=0, concat_axis=2, tiled=True)
    time_back = jnp.einsum(
        "ts,opti->opsi", time_factor, band_slab, preferred_element_type=f32
    ).astype(jnp.bfloat16)
    lat_back = jnp.einsum("opsi,ij->opsj", time_back, lat_factor, preferred_element_type=f32)
    return (flux_probes.astype(f32) + lat_back).astype(jnp.bfloat16)


def solution(mesh):
    in_specs = (
        P("lon", "groups", None, None),
        P(),
        P(),
        P(),
        P("lon", None, None),
        P("lon", None),
        P("lon"),
        P("lon"),
        P("lon", None),
    )
    out_specs = P("lon", "groups", None, None)
    return jax.shard_map(body, mesh=mesh, in_specs=in_specs, out_specs=out_specs, check_vma=False)
```

profile of v0, /device:TPU:13, one launch (start us, length us, event | category | flops | bytes accessed | tf_op | source)
XLA Modules:
  0.0 1261.3 jit_solution(17459995641494867938)
XLA Ops:
  6.5 19.1 %convert_bitcast_fusion.1 = bf16[48,4,192,256]{3,2,1,0:T(8,128)(2,1)} fusion(bf16[48,4,192,256]{3,2,1,0:T(8,128)(2,1)} %param.9, bf16[256,256]{1,0:T(8,128)(2,1)} %param.11, bf16[192,192]{1,0:T(8,128)(2,1)} %param.10), kind=kOutput, calls=%fused_computation.11 | convolution fusion | flops 8474591232 | bytes 37953536 | tf_op jit(solution)/shard_map/ts,opsi->opti/dot_general | solution.py:30
  25.6 24.8 %copy.29 = bf16[48,4,192,256]{3,1,0,2:T(4,128)(2,1)} copy(bf16[48,4,192,256]{3,2,1,0:T(8,128)(2,1)} %convert_bitcast_fusion.1) | data formatting | bytes 37748736 | tf_op jit(solution)/shard_map/convert_element_type | solution.py:32
  50.4 0.0 copy-start.10
  50.4 6.7 all-to-all-start
  57.1 0.2 all-reduce.3.cloned.1.call-start
  57.4 406.8 %all-to-all-done = bf16[48,4,192,256]{3,1,0,2:T(4,128)(2,1)} async-done(((bf16[48,4,192,256]{3,1,0,2:T(4,128)(2,1)}), bf16[48,4,192,256]{3,1,0,2:T(4,128)(2,1)}, u32[]{:S(2)}, u32[]{:S(2)}) %all-to-all-start) | async-done | bytes 18874400 | tf_op jit(solution)/shard_map/all_to_all | solution.py:33
  464.2 11.1 copy.30
  475.3 0.0 copy-start.6
  475.3 6.8 copy.31
  482.1 24.9 %convolution_convert_fusion = bf16[4,12,256,768]{3,2,1,0:T(8,128)(2,1)} fusion(bf16[768,4,12,256]{3,0,2,1:T(8,128)(2,1)} %bitcast.93, bf16[768,768]{1,0:T(8,128)(2,1)S(1)} %copy-done.6), kind=kOutput, calls=%fused_computation.15 | convolution fusion | flops 14504951808 | bytes 38928384 | tf_op jit(solution)/shard_map/ko,optl->kptl/dot_general | solution.py:34
  507.0 31.9 %copy.33 = bf16[768,4,12,2,128]{4,1,3,2,0:T(4,128)(2,1)} copy(bf16[768,4,12,2,128]{0,4,3,2,1:T(8,128)(2,1)} %bitcast.94) | data formatting | bytes 37748736 | tf_op jit(solution)/shard_map/reshape | solution.py:40
  538.9 7.2 gather_fusion
  546.1 1.2 fusion.33
  547.3 2.7 scatter_fusion
  550.1 0.7 copy-done.2
  550.8 0.0 all-reduce.3.cloned.1.call-update
  550.8 0.7 dynamic-slice
  552.2 86.2 %all-reduce.3.cloned.1.call-done = f32[128,4,128]{2,1,0:T(4,128)} async-done(((f32[128,4,128]{2,1,0:T(4,128)}), f32[128,4,128]{2,1,0:T(4,128)}) %all-reduce.3.cloned.1.call-update) | async-done | bytes 262160
  638.4 0.7 fusion.25
  639.1 17.4 %all_gather.3 = bf16[128,4,128]{2,1,0:T(4,128)(2,1)S(1)} all-gather(bf16[8,4,128]{2,1,0:T(4,128)(2,1)S(1)} %fusion.25), channel_id=1, replica_groups=mesh['groups'=2,'lon'=16] {'lon'}, dimensions={0}, use_global_device_ids=true | all-gather | bytes 139264 | tf_op jit(solution)/shard_map/all_gather | solution.py:50
  656.5 0.7 gather_fusion.1
  657.2 0.7 fusion.34
  657.8 12.6 %broadcast_in_dim.23 = f32[768,4,12,2,128]{4,1,3,2,0:T(4,128)} broadcast(f32[]{:T(128)} %constant.42.clone.1), dimensions={} | broadcast | bytes 37748740 | tf_op jit(solution)/shard_map/broadcast_in_dim | solution.py:54
  670.5 6.9 scatter_fusion.1
  677.3 19.6 %convert_element_type.49 = bf16[768,4,12,2,128]{4,1,3,2,0:T(4,128)(2,1)} convert(f32[768,4,12,2,128]{4,1,3,2,0:T(4,128)} %scatter_fusion.1) | non-fusion elementwise | flops 9437184 | bytes 56623104 | tf_op jit(solution)/shard_map/convert_element_type | solution.py:58
  696.9 30.1 %copy.34 = bf16[768,4,12,2,128]{0,4,3,2,1:T(8,128)(2,1)} copy(bf16[768,4,12,2,128]{4,1,3,2,0:T(4,128)(2,1)} %convert_element_type.49) | data formatting | bytes 37748736 | tf_op jit(solution)/shard_map/convert_element_type | solution.py:58
  727.1 24.4 %convert_bitcast_fusion = bf16[768,4,12,256]{0,3,2,1:T(8,128)(2,1)} fusion(bf16[768,4,12,256]{0,3,2,1:T(8,128)(2,1)} %bitcast.95, bf16[768,768]{1,0:T(8,128)(2,1)S(1)} %copy-done.7), kind=kOutput, calls=%fused_computation.10 | convolution fusion | flops 14504951808 | bytes 38928384 | tf_op jit(solution)/shard_map/ko,kptl->optl/dot_general | solution.py:59
  751.5 32.0 %copy.35 = bf16[768,4,12,256]{3,1,2,0:T(4,128)(2,1)} copy(bf16[768,4,12,256]{0,3,2,1:T(8,128)(2,1)} %convert_bitcast_fusion) | data formatting | bytes 37748736 | tf_op jit(solution)/shard_map/convert_element_type | solution.py:61
  783.5 416.5 %all_to_all.36 = bf16[768,4,12,256]{3,1,2,0:T(4,128)(2,1)S(1)} all-to-all(bf16[768,4,12,256]{3,1,2,0:T(4,128)(2,1)} %copy.35), channel_id=1, replica_groups=mesh['groups'=2,'lon'=16] {'lon'}, dimensions={0} | all-to-all | bytes 37748736 | tf_op jit(solution)/shard_map/all_to_all | solution.py:62
  1200.0 18.7 %copy.36 = bf16[768,4,12,256]{3,0,2,1:T(8,128)(2,1)S(1)} copy(bf16[768,4,12,256]{3,1,2,0:T(4,128)(2,1)S(1)} %all_to_all.36) | data formatting | bytes 37748736 | tf_op jit(solution)/shard_map/all_to_all | solution.py:62
  1218.7 7.0 copy.37
  1225.7 28.7 %add_convert_fusion = bf16[48,4,192,256]{3,2,1,0:T(8,128)(2,1)} fusion(bf16[48,4,192,256]{3,2,1,0:T(8,128)(2,1)} %param.9, bf16[48,4,192,256]{3,0,2,1:T(8,128)(2,1)} %bitcast.96, bf16[256,256]{1,0:T(8,128)(2,1)S(1)} %copy-done.3, bf16[192,192]{1,0:T(8,128)(2,1)S(1)} %copy-done.4), kind=kOutput, calls=%fused_computation.4 | convolution fusion | flops 8493465600 | bytes 56827904 | tf_op jit(solution)/shard_map/opsi,ij->opsj/dot_general | solution.py:66
  (25 shorter events, 0.1 us)
Async XLA Ops:
  6.5 539.6 %copy-start = (bf16[64,128,128]{2,1,0:T(8,128)(2,1)S(1)}, bf16[64,128,128]{2,1,0:T(8,128)(2,1)}, u32[]{:S(2)}) copy-start(bf16[64,128,128]{2,1,0:T(8,128)(2,1)} %param.13) | copy-start | bytes 6291460
  50.4 6.9 copy-start.8
  50.4 7.0 copy-start.9
  50.4 7.0 copy-start.10
  50.4 413.8 %all-to-all-start = ((bf16[48,4,192,256]{3,1,0,2:T(4,128)(2,1)}), bf16[48,4,192,256]{3,1,0,2:T(4,128)(2,1)}, u32[]{:S(2)}, u32[]{:S(2)}) async-start(bf16[48,4,192,256]{3,1,0,2:T(4,128)(2,1)} %copy.29), calls=%async_computation | async-start | bytes 37748736 | tf_op jit(solution)/shard_map/all_to_all | solution.py:33
  57.1 581.3 %all-reduce.3.cloned.1.call-start = ((), (), s32[]{:S(2)}) async-start(), calls=%async_computation.2 | async-start | bytes 524288
  475.3 6.8 copy-start.6
  507.0 43.8 %copy-start.11 = (u32[32]{0:T(128)S(1)}, u32[32]{0:T(128)}, u32[]{:S(2)}) copy-start(u32[32]{0:T(128)} %constant.96) | copy-start | bytes 388
  507.0 131.4 %copy-start.5 = (f32[8,128]{1,0:T(8,128)S(1)}, f32[8,128]{1,0:T(8,128)}, u32[]{:S(2)}) copy-start(f32[8,128]{1,0:T(8,128)} %param.17) | copy-start | bytes 12292
  550.1 0.7 copy-start.2
  696.9 30.1 %copy-start.7 = (bf16[768,768]{1,0:T(8,128)(2,1)S(1)}, bf16[768,768]{1,0:T(8,128)(2,1)}, u32[]{:S(2)}) copy-start(bf16[768,768]{1,0:T(8,128)(2,1)} %param.12) | copy-start | bytes 3538948
  1218.7 7.0 copy-start.3
  1218.7 7.0 copy-start.4
  1225.7 28.7 %copy-start.1 = (bf16[64,128,128]{2,1,0:T(8,128)(2,1)S(1)}, bf16[64,128,128]{2,1,0:T(8,128)(2,1)}, u32[]{:S(2)}) copy-start(bf16[64,128,128]{2,1,0:T(8,128)(2,1)} %param.13) | copy-start | bytes 6291460
Sparse Core Ops, SparseCore 0:
  550.9 87.4 all-reduce.2
where the time goes:
time: 1270 us; the launch traced here: 1260 us
  waiting for transfers between devices  493 us (39%)
  blocking collectives  434 us (34%)
  local copies, waits for them, and re-layouts  184 us (14%)
  matrix products  98.9 us (8%)
  other arithmetic  30 us (2%)
  between operations  14.2 us (1%)
    all_to_all x1, blocking collectives, body(): lax.all_to_all(lon_back, 'lon', split_axis=0, concat_axis=2, tiled=True)  416 us
    all_to_all x1, waiting for transfers between devices, body(): lax.all_to_all(time_mixed, 'lon', split_axis=2, concat_axis=0, tiled=True)  407 us
    unnamed x2, waiting for transfers between devices  86.2 us
    convert_element_type x1, local copies, waits for them, and re-layouts, body(): lon_back = jnp.einsum('ko,kptl->optl', lon_factor, adjoint_field, preferr...  32 us
    reshape x1, local copies, waits for them, and re-layouts, body(): shaped = prior_field.reshape(longitudes, probe_count, day_dev, bands, SND)  31.9 us
    convert_element_type x1, local copies, waits for them, and re-layouts, body(): adjoint.reshape(longitudes, probe_count, day_dev, lats).astype(jnp.bfloat16)  30.1 us
    dot_general x1, matrix products, body(): jnp.einsum('opsi,ij->opsj', time_back, lat_factor, preferred_element_type...  28.7 us
    all_to_all x2, local copies, waits for them, and re-layouts, body(): lax.all_to_all(lon_back, 'lon', split_axis=0, concat_axis=2, tiled=True)  25.7 us
  transfers between devices with their start and end apart: 2, of which 2 were waited for; matrix products, arithmetic and copies ran while one was open for 0% of the time, Pallas kernels for 0%

commit v1 on v0

v1 whole, which is shorter than its diff:
```python
import functools

import jax
import jax.numpy as jnp
from jax import lax
from jax.experimental import pallas as pl
from jax.experimental.pallas import tpu as pltpu
from jax.sharding import PartitionSpec as P

SND = 128
GROUPS = 16
PAD = 16
f32 = jnp.float32
bf16 = jnp.bfloat16
VMEM_LIMIT = 60 * 1024 * 1024


def entry_barrier(n):
    me = lax.axis_index("lon")
    barrier = pltpu.get_barrier_semaphore()

    def greet(off, carry):
        pl.semaphore_signal(
            barrier,
            inc=1,
            device_id={"lon": lax.rem(me + off, n)},
            device_id_type=pl.DeviceIdType.MESH,
        )
        return carry

    lax.fori_loop(1, n, greet, 0)
    pl.semaphore_wait(barrier, n - 1)


def gather_kernel(n, x_ref, out_ref, send_sem, recv_sem):
    me = lax.axis_index("lon")
    entry_barrier(n)

    def push(off):
        return pltpu.make_async_remote_copy(
            src_ref=x_ref,
            dst_ref=out_ref.at[me],
            send_sem=send_sem.at[off],
            recv_sem=recv_sem.at[off],
            device_id={"lon": lax.rem(me + off, n)},
            device_id_type=pl.DeviceIdType.MESH,
        )

    def start(off, carry):
        push(off).start()
        return carry

    def finish(off, carry):
        push(off).wait()
        return carry

    lax.fori_loop(1, n, start, 0)
    out_ref[me] = x_ref[...]
    lax.fori_loop(1, n, finish, 0)


def gather(x, n, collective_id):
    return pl.pallas_call(
        functools.partial(gather_kernel, n),
        out_shape=jax.ShapeDtypeStruct((n,) + x.shape, x.dtype),
        in_specs=[pl.BlockSpec(memory_space=pltpu.VMEM)],
        out_specs=pl.BlockSpec(memory_space=pltpu.VMEM),
        scratch_shapes=[pltpu.SemaphoreType.DMA((n,)), pltpu.SemaphoreType.DMA((n,))],
        compiler_params=pltpu.CompilerParams(
            collective_id=collective_id, has_side_effects=True, vmem_limit_bytes=VMEM_LIMIT
        ),
    )(x)


def scatter_sum(n, x_ref, held, send_sem, recv_sem):
    me = lax.axis_index("lon")

    def push(off):
        peer = lax.rem(me + off, n)
        return pltpu.make_async_remote_copy(
            src_ref=x_ref.at[peer],
            dst_ref=held.at[me],
            send_sem=send_sem.at[off],
            recv_sem=recv_sem.at[off],
            device_id={"lon": peer},
            device_id_type=pl.DeviceIdType.MESH,
        )

    def start(off, carry):
        push(off).start()
        return carry

    def finish(off, total):
        push(off).wait()
        return total + held[lax.rem(me - off + n, n)]

    lax.fori_loop(1, n, start, 0)
    return finish, x_ref[me]


def reduce_kernel(n, x_ref, out_ref, held, send_sem, recv_sem):
    entry_barrier(n)
    finish, own = scatter_sum(n, x_ref, held, send_sem, recv_sem)
    out_ref[...] = own
    me = lax.axis_index("lon")

    def add(off, carry):
        out_ref[...] = finish(off, out_ref[...])
        return carry

    lax.fori_loop(1, n, add, 0)


def reduce_blocks(x, n, collective_id):
    return pl.pallas_call(
        functools.partial(reduce_kernel, n),
        out_shape=jax.ShapeDtypeStruct(x.shape[1:], x.dtype),
        in_specs=[pl.BlockSpec(memory_space=pltpu.VMEM)],
        out_specs=pl.BlockSpec(memory_space=pltpu.VMEM),
        scratch_shapes=[
            pltpu.VMEM(x.shape, x.dtype),
            pltpu.SemaphoreType.DMA((n,)),
            pltpu.SemaphoreType.DMA((n,)),
        ],
        compiler_params=pltpu.CompilerParams(
            collective_id=collective_id, has_side_effects=True, vmem_limit_bytes=VMEM_LIMIT
        ),
    )(x)


def residual_kernel(n, x_ref, w_ref, out_ref, held, mine, send_sem, recv_sem, send2, recv2):
    entry_barrier(n)
    me = lax.axis_index("lon")
    finish, own = scatter_sum(n, x_ref, held, send_sem, recv_sem)
    total = lax.fori_loop(1, n, finish, own)
    mine[...] = (w_ref[...] * total).astype(bf16).astype(f32)

    def push(off):
        return pltpu.make_async_remote_copy(
            src_ref=mine,
            dst_ref=out_ref.at[me],
            send_sem=send2.at[off],
            recv_sem=recv2.at[off],
            device_id={"lon": lax.rem(me + off, n)},
            device_id_type=pl.DeviceIdType.MESH,
        )

    def start(off, carry):
        push(off).start()
        return carry

    def done(off, carry):
        push(off).wait()
        return carry

    lax.fori_loop(1, n, start, 0)
    out_ref[me] = mine[...]
    lax.fori_loop(1, n, done, 0)


def residuals(x, weights, n, collective_id):
    sems = [pltpu.SemaphoreType.DMA((n,))] * 4
    return pl.pallas_call(
        functools.partial(residual_kernel, n),
        out_shape=jax.ShapeDtypeStruct(x.shape, x.dtype),
        in_specs=[pl.BlockSpec(memory_space=pltpu.VMEM)] * 2,
        out_specs=pl.BlockSpec(memory_space=pltpu.VMEM),
        scratch_shapes=[pltpu.VMEM(x.shape, x.dtype), pltpu.VMEM(x.shape[1:], x.dtype)] + sems,
        compiler_params=pltpu.CompilerParams(
            collective_id=collective_id, has_side_effects=True, vmem_limit_bytes=VMEM_LIMIT
        ),
    )(x, weights)


def forward_kernel(flux_ref, time_ref, sel_ref, lat_ref, band_ref, out_ref, mixed, total):
    chunk, probes, days, lats = flux_ref.shape
    tiles = band_ref.shape[1]
    step = pl.program_id(0)

    @pl.when(step == 0)
    def _():
        total[...] = jnp.zeros_like(total)

    def mix(o, carry):
        rows = pl.ds(pl.multiple_of(o * PAD, PAD), PAD)
        for p in range(probes):
            t = jnp.dot(time_ref[...], flux_ref[o, p], preferred_element_type=f32)
            mixed[p, :, rows, :] = t.astype(bf16).reshape(GROUPS, PAD, lats)
        return carry

    lax.fori_loop(0, chunk, mix, 0)

    def pick(g, carry):
        for p in range(probes):
            total[g, p] += jnp.dot(sel_ref[g], mixed[p, g], preferred_element_type=f32)
        return carry

    lax.fori_loop(0, GROUPS, pick, 0)

    @pl.when(step == pl.num_programs(0) - 1)
    def _():
        def last(g, carry):
            upper = jnp.broadcast_to(band_ref[g], (tiles, SND)) > 0
            for p in range(probes):
                z = jnp.dot(total[g, p].astype(bf16), lat_ref[...], preferred_element_type=f32)
                out_ref[g, :, p * SND : (p + 1) * SND] = jnp.where(upper, z[:, SND:], z[:, :SND])
            return carry

        lax.fori_loop(0, GROUPS, last, 0)


def backward_kernel(flux_ref, time_ref, sel_ref, back_ref, out_ref, mixed):
    chunk, probes, days, lats = flux_ref.shape

    def spread(g, carry):
        for p in range(probes):
            mixed[p, g] = jnp.dot(
                sel_ref[g], back_ref[p, g], preferred_element_type=f32
            ).astype(bf16)
        return carry

    lax.fori_loop(0, GROUPS, spread, 0)

    def mix(o, carry):
        rows = pl.ds(pl.multiple_of(o * PAD, PAD), PAD)
        for p in range(probes):
            held = mixed[p, :, rows, :].reshape(GROUPS * PAD, lats)
            t = jnp.dot(time_ref[...], held, preferred_element_type=f32)
            out_ref[o, p] = (flux_ref[o, p].astype(f32) + t).astype(bf16)
        return carry

    lax.fori_loop(0, chunk, mix, 0)


def body(
    flux_probes,
    time_factor,
    lat_factor,
    lon_factor,
    footprint,
    entry_owner,
    entry_block,
    entry_tile,
    obs_weight,
):
    n = lax.axis_size("lon")
    me = lax.axis_index("lon")
    lon_dev, probes, days, lats = flux_probes.shape
    longitudes = lon_factor.shape[0]
    bands = lats // SND
    day_dev = days // n
    blocks_dev = obs_weight.shape[0]
    entries = entry_tile.shape[0]
    tiles = entries * n // GROUPS
    span = days // GROUPS
    chunk = max(c for c in range(1, 17) if lon_dev % c == 0)

    padded = jnp.pad(entry_tile[None, :], ((0, 7), (0, -entries % 128)))
    tile_all = gather(padded, n, 0)[:, 0, :entries]
    day = jnp.arange(n, dtype=jnp.int32)[:, None] * day_dev + tile_all // bands % day_dev
    lon_of = (tile_all // (day_dev * bands)).reshape(GROUPS, tiles)
    slot = (day % span).reshape(GROUPS, tiles)
    band_of = (tile_all % bands).reshape(GROUPS, tiles)

    time_pad = jnp.pad(
        time_factor.reshape(GROUPS, span, days), ((0, 0), (0, PAD - span), (0, 0))
    ).reshape(GROUPS * PAD, days)

    wide = lon_dev * PAD
    columns = lax.dynamic_slice_in_dim(lon_factor, me * lon_dev, lon_dev, axis=1)
    repeat = (
        jnp.arange(lon_dev, dtype=jnp.int32)[:, None]
        == jnp.arange(wide, dtype=jnp.int32)[None, :] // PAD
    ).astype(bf16)
    lon_wide = jnp.dot(columns, repeat, preferred_element_type=f32).astype(bf16)
    hot = (lon_of[:, :, None] == jnp.arange(longitudes, dtype=jnp.int32)).astype(bf16)
    row_slot = jnp.arange(wide, dtype=jnp.int32) % PAD
    sel = jnp.einsum("gek,kr->ger", hot, lon_wide, preferred_element_type=f32)
    sel = jnp.where(slot[:, :, None] == row_slot, sel, 0.0).astype(bf16)
    sel_t = jnp.einsum("kr,gek->gre", lon_wide, hot, preferred_element_type=f32)
    sel_t = jnp.where(slot[:, None, :] == row_slot[None, :, None], sel_t, 0.0).astype(bf16)

    steps = lon_dev // chunk
    flux_spec = pl.BlockSpec((chunk, probes, days, lats), lambda i: (i, 0, 0, 0))
    mixed_shape = pltpu.VMEM((probes, GROUPS, chunk * PAD, lats), bf16)
    share = pl.pallas_call(
        forward_kernel,
        grid=(steps,),
        out_shape=jax.ShapeDtypeStruct((GROUPS, tiles, probes * SND), f32),
        in_specs=[
            flux_spec,
            pl.BlockSpec((GROUPS * PAD, days), lambda i: (0, 0)),
            pl.BlockSpec((GROUPS, tiles, chunk * PAD), lambda i: (0, 0, i)),
            pl.BlockSpec((lats, lats), lambda i: (0, 0)),
            pl.BlockSpec((GROUPS, tiles, 1), lambda i: (0, 0, 0)),
        ],
        out_specs=pl.BlockSpec((GROUPS, tiles, probes * SND), lambda i: (0, 0, 0)),
        scratch_shapes=[mixed_shape, pltpu.VMEM((GROUPS, probes, tiles, lats), f32)],
        compiler_params=pltpu.CompilerParams(vmem_limit_bytes=VMEM_LIMIT),
    )(flux_probes, time_pad, sel, lat_factor.T, band_of[:, :, None])

    values = reduce_blocks(share.reshape(n, entries, probes * SND), n, 1)
    tile_values = values.astype(bf16).reshape(entries, probes, SND)
    partial = jnp.einsum("erc,epc->epr", footprint, tile_values, preferred_element_type=f32)
    block = entry_owner[:, 0] * blocks_dev + entry_block
    named = jnp.arange(n * blocks_dev, dtype=jnp.int32)[:, None] == block[None, :]
    sums = jnp.dot(
        named.astype(f32),
        partial.reshape(entries, probes * SND),
        precision=lax.Precision.HIGHEST,
        preferred_element_type=f32,
    )
    weights = jnp.tile(obs_weight, (1, probes))
    weighted = residuals(sums.reshape(n, blocks_dev, probes * SND), weights, n, 2)
    weighted = weighted.reshape(n * blocks_dev, probes * SND).astype(bf16)
    resid = jnp.einsum("be,bx->ex", named.astype(bf16), weighted, preferred_element_type=f32)
    resid = resid.astype(bf16).reshape(entries, probes, SND)
    back = jnp.einsum("erc,epr->epc", footprint, resid, preferred_element_type=f32)
    back = back.astype(bf16).reshape(entries, probes * SND)
    back_all = gather(back, n, 3).reshape(GROUPS, tiles, probes, SND)
    placed = jnp.concatenate(
        [jnp.where(band_of[:, :, None, None] == b, back_all, 0) for b in range(bands)], axis=-1
    )
    back_lat = jnp.einsum(
        "gepi,ij->pgej", placed, lat_factor, preferred_element_type=f32
    ).astype(bf16)

    return pl.pallas_call(
        backward_kernel,
        grid=(steps,),
        out_shape=jax.ShapeDtypeStruct(flux_probes.shape, bf16),
        in_specs=[
            flux_spec,
            pl.BlockSpec((days, GROUPS * PAD), lambda i: (0, 0)),
            pl.BlockSpec((GROUPS, chunk * PAD, tiles), lambda i: (0, i, 0)),
            pl.BlockSpec((probes, GROUPS, tiles, lats), lambda i: (0, 0, 0, 0)),
        ],
        out_specs=flux_spec,
        scratch_shapes=[mixed_shape],
        compiler_params=pltpu.CompilerParams(vmem_limit_bytes=VMEM_LIMIT),
    )(flux_probes, time_pad.T, sel_t, back_lat)


def solution(mesh):
    in_specs = (
        P("lon", "groups", None, None),
        P(),
        P(),
        P(),
        P("lon", None, None),
        P("lon", None),
        P("lon"),
        P("lon"),
        P("lon", None),
    )
    out_specs = P("lon", "groups", None, None)
    return jax.shard_map(body, mesh=mesh, in_specs=in_specs, out_specs=out_specs, check_vma=False)
```

time: 1270 us -> 206 us (0.16)
  waiting for transfers between devices: 493 us -> 0 us
  blocking collectives: 434 us -> 0 us
  Pallas kernels: 0 us -> 174 us
  local copies, waits for them, and re-layouts: 184 us -> 11 us
  matrix products: 98.9 us -> 10.6 us
  other arithmetic: 30 us -> 10.1 us
  between operations: 14.2 us -> 0.12 us
    all_to_all x1 -> x0, blocking collectives: 416 us -> none  [body(): lax.all_to_all(lon_back, 'lon', split_axis=0, concat_axis=2, tiled=True)]
    all_to_all x1 -> x0, waiting for transfers between devices: 407 us -> none  [body(): lax.all_to_all(time_mixed, 'lon', split_axis=2, concat_axis=0, tiled=True)]
    pallas_call x0 -> x6, Pallas kernels: none -> 174 us  [the longest x1 52.3 us: reduce_blocks(): pl.pallas_call(functools.partial(reduce_kernel, n), out_shape=jax.ShapeDt...]
    dot_general x5, matrix products: 97.7 us -> 9.4 us  [the longest x1 4.52 us: body(): sel_t = jnp.einsum('kr,gek->gre', lon_wide, hot, preferred_element_type=f32)]
    convert_element_type x3 -> x0, local copies, waits for them, and re-layouts: 87 us -> none  [the longest x1 32 us: body(): lon_back = jnp.einsum('ko,kptl->optl', lon_factor, adjoint_field, preferr...]
    unnamed x2 -> x0, waiting for transfers between devices: 86.2 us -> none
    all_to_all x4 -> x0, local copies, waits for them, and re-layouts: 43.6 us -> none  [the longest x2 25.7 us: body(): lax.all_to_all(lon_back, 'lon', split_axis=0, concat_axis=2, tiled=True)]
    reshape x1 -> x5, local copies, waits for them, and re-layouts: 31.9 us -> 1.8 us  [the longest x1 0.93 us: body(): time_factor.reshape(GROUPS, span, days)]
  transfers between devices with their start and end apart: 2 -> 0, of which waited for: 2 -> 0; matrix products, arithmetic and copies ran while one was open for 0% -> 0% of each run, Pallas kernels for 0% -> 0%
where the time goes in v1:
time: 206 us
  Pallas kernels  174 us (84%)
  local copies, waits for them, and re-layouts  11 us (5%)
  matrix products  10.6 us (5%)
  other arithmetic  10.1 us (5%)
    pallas_call x1, Pallas kernels, reduce_blocks(): pl.pallas_call(functools.partial(reduce_kernel, n), out_shape=jax.ShapeDt...  52.3 us
    pallas_call x2, Pallas kernels, gather(): pl.pallas_call(functools.partial(gather_kernel, n), out_shape=jax.ShapeDt...  38.1 us
    pallas_call x1, Pallas kernels, body(): pl.pallas_call(backward_kernel, grid=(steps,), out_shape=jax.ShapeDtypeSt...  32.6 us
    pallas_call x1, Pallas kernels, body(): pl.pallas_call(forward_kernel, grid=(steps,), out_shape=jax.ShapeDtypeStr...  32.3 us
    pallas_call x1, Pallas kernels, residuals(): pl.pallas_call(functools.partial(residual_kernel, n), out_shape=jax.Shape...  18.7 us
    convert_element_type x1, other arithmetic, body(): jnp.where(slot[:, None, :] == row_slot[None, :, None], sel_t, 0.0)  4.55 us
    dot_general x1, matrix products, body(): sel_t = jnp.einsum('kr,gek->gre', lon_wide, hot, preferred_element_type=f32)  4.52 us
    dot_general x1, local copies, waits for them, and re-layouts, body(): sel_t = jnp.einsum('kr,gek->gre', lon_wide, hot, preferred_element_type=f32)  4.13 us

profile of v1, /device:TPU:13, one launch (start us, length us, event | category | flops | bytes accessed | tf_op | source)
XLA Modules:
  0.0 205.9 jit_solution(7035491867868641376)
XLA Ops:
  0.0 0.0 copy-start
  0.0 0.8 bitcast_add_fusion
  0.8 1.3 pad.9.x_ref
  2.1 1.3 broadcast_bitcast_fusion.w_ref
  3.4 8.5 %shard_map.91 = s32[16,8,128]{2,1,0:T(8,128)} custom-call(s32[8,128]{1,0:T(8,128)} %pad.9.x_ref), custom_call_target="tpu_custom_call" | custom-call | tf_op jit(solution)/shard_map/pallas_call | solution.py:63
  11.9 1.0 and_select_fusion
  12.9 0.1 add_select_fusion.1
  13.0 0.9 reshape.268
  13.9 0.0 copy-start.1
  14.0 0.8 copy.18
  14.7 1.7 copy.20
  16.4 0.2 copy.21
  16.6 1.0 add_select_fusion.band_ref
  17.6 4.5 %select_convert_fusion = (bf16[16,64,768]{2,1,0:T(8,128)(2,1)}, bf16[16,64,768]{2,1,0:T(8,128)(2,1)}) fusion(s32[768]{0:T(1024)S(1)} %get-tuple-element.16, s32[16,64]{1,0:T(8,128)S(1)} %get-tuple-element.11, bf16[768,768]{1,0:T(8,128)(2,1)} %param.12, s32[]{:T(128)S(6)} %select_n.113, s32[768]{0:T(1024)S(1)} %get-tuple-element.15, ...), kind=kOutput, calls=%fused_computation.2 | convolution fusion | flops 1267568640 | bytes 3356676 | tf_op jit(solution)/shard_map/kr,gek->gre/dot_general | solution.py:280
  22.1 0.0 copy-done.1
  22.1 32.3 %shard_map.92.x_ref = f32[16,64,512]{2,1,0:T(8,128)} custom-call(bf16[48,4,192,256]{3,2,1,0:T(8,128)(2,1)} %flux_ref.3, bf16[256,192]{1,0:T(8,128)(2,1)} %bitcast.45, bf16[16,64,768]{2,1,0:T(8,128)(2,1)} %get-tuple-element.13.sel_ref, bf16[256,256]{1,0:T(8,128)(2,1)} %bitcast.46, s32[16,64,1]{2,1,0:T(8,128)} %add_select_fusion.band_ref), custom_call_target="tpu_custom_call" | custom-call | tf_op jit(solution)/shard_map/pallas_call | solution.py:286
  54.4 52.3 %shard_map.93 = f32[64,512]{1,0:T(8,128)} custom-call(f32[16,64,512]{2,1,0:T(8,128)} %shard_map.92.x_ref), custom_call_target="tpu_custom_call" | custom-call | tf_op jit(solution)/shard_map/pallas_call | solution.py:115
  106.7 0.9 convert_element_type.41
  107.7 0.0 copy-done
  107.7 1.2 fusion.37
  108.9 0.1 reshape.276
  109.0 1.0 fusion.16.x_ref
  110.0 18.7 %shard_map.94 = f32[16,8,512]{2,1,0:T(8,128)} custom-call(f32[16,8,512]{2,1,0:T(8,128)} %fusion.16.x_ref, f32[8,512]{1,0:T(8,128)} %broadcast_bitcast_fusion.w_ref), custom_call_target="tpu_custom_call" | custom-call | tf_op jit(solution)/shard_map/pallas_call | solution.py:163
  128.7 1.2 convolution_convert_fusion.2
  129.9 0.7 convolution_convert_fusion.1
  130.6 0.6 copy.38
  131.2 29.6 %shard_map.95 = bf16[16,64,512]{2,1,0:T(8,128)(2,1)} custom-call(bf16[64,512]{1,0:T(8,128)(2,1)} %bitcast.49), custom_call_target="tpu_custom_call" | custom-call | tf_op jit(solution)/shard_map/pallas_call | solution.py:63
  160.8 1.8 bitcast_select_fusion.2
  162.6 2.1 convert_bitcast_fusion.back_ref
  164.6 4.1 %copy.19 = bf16[16,64,768]{1,2,0:T(8,128)(2,1)} copy(bf16[16,64,768]{2,1,0:T(8,128)(2,1)} %get-tuple-element.14) | data formatting | bytes 3145728 | tf_op jit(solution)/shard_map/kr,gek->gre/dot_general | solution.py:280
  168.8 4.6 %fusion.sel_ref = bf16[16,768,64]{2,1,0:T(8,128)(2,1)} fusion(bf16[16,64,768]{1,2,0:T(8,128)(2,1)} %copy.19, s32[16,64]{1,0:T(8,128)S(1)} %bitcast.53, s32[768]{0:T(1024)S(1)} %get-tuple-element.16), kind=kLoop, calls=%fused_computation.1 | loop fusion | flops 1572864 | bytes 3152896 | tf_op jit(solution)/shard_map/convert_element_type | solution.py:281
  173.3 32.6 %shard_map.96 = bf16[48,4,192,256]{3,2,1,0:T(8,128)(2,1)} custom-call(bf16[48,4,192,256]{3,2,1,0:T(8,128)(2,1)} %flux_ref.3, bf16[192,256]{1,0:T(8,128)(2,1)} %bitcast.47, bf16[16,768,64]{2,1,0:T(8,128)(2,1)} %fusion.sel_ref, bf16[4,16,64,256]{3,2,1,0:T(8,128)(2,1)} %convert_bitcast_fusion.back_ref), custom_call_target="tpu_custom_call" | custom-call | tf_op jit(solution)/shard_map/pallas_call | solution.py:328
  (9 shorter events, 0.1 us)
Async XLA Ops:
  0.0 107.7 %copy-start = (bf16[64,128,128]{2,1,0:T(8,128)(2,1)S(1)}, bf16[64,128,128]{2,1,0:T(8,128)(2,1)}, u32[]{:S(2)}) copy-start(bf16[64,128,128]{2,1,0:T(8,128)(2,1)} %param.13) | copy-start | bytes 6291460
  13.9 8.2 %copy-start.1 = (bf16[16,16,192]{2,1,0:T(8,128)(2,1)}, bf16[16,16,192]{2,1,0:T(8,128)(2,1)S(1)}, u32[]{:S(2)}) copy-start(bf16[16,16,192]{2,1,0:T(8,128)(2,1)S(1)} %pad.8) | copy-start | bytes 294916
  131.2 31.4 %copy-start.2 = (bf16[256,256]{1,0:T(8,128)(2,1)S(1)}, bf16[256,256]{1,0:T(8,128)(2,1)}, u32[]{:S(2)}) copy-start(bf16[256,256]{1,0:T(8,128)(2,1)} %param.11) | copy-start | bytes 393220

commit v2 on v1

--- a/solution.py
+++ b/solution.py
@@ -92,10 +92,10 @@
 
     def finish(off, total):
         push(off).wait()
-        return total + held[lax.rem(me - off + n, n)]
+        return total + held[lax.rem(me - off + n, n)].astype(f32)
 
     lax.fori_loop(1, n, start, 0)
-    return finish, x_ref[me]
+    return finish, x_ref[me].astype(f32)
 
 
 def reduce_kernel(n, x_ref, out_ref, held, send_sem, recv_sem):
@@ -114,7 +114,7 @@
 def reduce_blocks(x, n, collective_id):
     return pl.pallas_call(
         functools.partial(reduce_kernel, n),
-        out_shape=jax.ShapeDtypeStruct(x.shape[1:], x.dtype),
+        out_shape=jax.ShapeDtypeStruct(x.shape[1:], f32),
         in_specs=[pl.BlockSpec(memory_space=pltpu.VMEM)],
         out_specs=pl.BlockSpec(memory_space=pltpu.VMEM),
         scratch_shapes=[
@@ -172,6 +172,18 @@
     )(x, weights)
 
 
+def repeat(count, probes, step):
+    width = max(w for w in range(1, 5) if count % w == 0)
+
+    def several(i, carry):
+        for q in range(width):
+            for p in range(probes):
+                step(i * width + q, p)
+        return carry
+
+    lax.fori_loop(0, count // width, several, 0)
+
+
 def forward_kernel(flux_ref, time_ref, sel_ref, lat_ref, band_ref, out_ref, mixed, total):
     chunk, probes, days, lats = flux_ref.shape
     tiles = band_ref.shape[1]
@@ -181,21 +193,17 @@
     def _():
         total[...] = jnp.zeros_like(total)
 
-    def mix(o, carry):
+    def mix(o, p):
         rows = pl.ds(pl.multiple_of(o * PAD, PAD), PAD)
-        for p in range(probes):
-            t = jnp.dot(time_ref[...], flux_ref[o, p], preferred_element_type=f32)
-            mixed[p, :, rows, :] = t.astype(bf16).reshape(GROUPS, PAD, lats)
-        return carry
-
-    lax.fori_loop(0, chunk, mix, 0)
-
-    def pick(g, carry):
-        for p in range(probes):
-            total[g, p] += jnp.dot(sel_ref[g], mixed[p, g], preferred_element_type=f32)
-        return carry
-
-    lax.fori_loop(0, GROUPS, pick, 0)
+        t = jnp.dot(time_ref[...], flux_ref[o, p], preferred_element_type=f32)
+        mixed[p, :, rows, :] = t.astype(bf16).reshape(GROUPS, PAD, lats)
+
+    repeat(chunk, probes, mix)
+
+    def pick(g, p):
+        total[g, p] += jnp.dot(sel_ref[g], mixed[p, g], preferred_element_type=f32)
+
+    repeat(GROUPS, probes, pick)
 
     @pl.when(step == pl.num_programs(0) - 1)
     def _():
@@ -203,7 +211,8 @@
             upper = jnp.broadcast_to(band_ref[g], (tiles, SND)) > 0
             for p in range(probes):
                 z = jnp.dot(total[g, p].astype(bf16), lat_ref[...], preferred_element_type=f32)
-                out_ref[g, :, p * SND : (p + 1) * SND] = jnp.where(upper, z[:, SND:], z[:, :SND])
+                half = jnp.where(upper, z[:, SND:], z[:, :SND])
+                out_ref[g, :, p * SND : (p + 1) * SND] = half.astype(bf16)
             return carry
 
         lax.fori_loop(0, GROUPS, last, 0)
@@ -213,23 +222,22 @@
     chunk, probes, days, lats = flux_ref.shape
 
     def spread(g, carry):
+        turned = jnp.transpose(sel_ref[g])
         for p in range(probes):
             mixed[p, g] = jnp.dot(
-                sel_ref[g], back_ref[p, g], preferred_element_type=f32
+                turned, back_ref[p, g], preferred_element_type=f32
             ).astype(bf16)
         return carry
 
     lax.fori_loop(0, GROUPS, spread, 0)
 
-    def mix(o, carry):
+    def mix(o, p):
         rows = pl.ds(pl.multiple_of(o * PAD, PAD), PAD)
-        for p in range(probes):
-            held = mixed[p, :, rows, :].reshape(GROUPS * PAD, lats)
-            t = jnp.dot(time_ref[...], held, preferred_element_type=f32)
-            out_ref[o, p] = (flux_ref[o, p].astype(f32) + t).astype(bf16)
-        return carry
-
-    lax.fori_loop(0, chunk, mix, 0)
+        held = mixed[p, :, rows, :].reshape(GROUPS * PAD, lats)
+        t = jnp.dot(time_ref[...], held, preferred_element_type=f32)
+        out_ref[o, p] = (flux_ref[o, p].astype(f32) + t).astype(bf16)
+
+    repeat(chunk, probes, mix)
 
 
 def body(
@@ -277,8 +285,6 @@
     row_slot = jnp.arange(wide, dtype=jnp.int32) % PAD
     sel = jnp.einsum("gek,kr->ger", hot, lon_wide, preferred_element_type=f32)
     sel = jnp.where(slot[:, :, None] == row_slot, sel, 0.0).astype(bf16)
-    sel_t = jnp.einsum("kr,gek->gre", lon_wide, hot, preferred_element_type=f32)
-    sel_t = jnp.where(slot[:, None, :] == row_slot[None, :, None], sel_t, 0.0).astype(bf16)
 
     steps = lon_dev // chunk
     flux_spec = pl.BlockSpec((chunk, probes, days, lats), lambda i: (i, 0, 0, 0))
@@ -286,7 +292,7 @@
     share = pl.pallas_call(
         forward_kernel,
         grid=(steps,),
-        out_shape=jax.ShapeDtypeStruct((GROUPS, tiles, probes * SND), f32),
+        out_shape=jax.ShapeDtypeStruct((GROUPS, tiles, probes * SND), bf16),
         in_specs=[
             flux_spec,
             pl.BlockSpec((GROUPS * PAD, days), lambda i: (0, 0)),
@@ -332,13 +338,13 @@
         in_specs=[
             flux_spec,
             pl.BlockSpec((days, GROUPS * PAD), lambda i: (0, 0)),
-            pl.BlockSpec((GROUPS, chunk * PAD, tiles), lambda i: (0, i, 0)),
+            pl.BlockSpec((GROUPS, tiles, chunk * PAD), lambda i: (0, 0, i)),
             pl.BlockSpec((probes, GROUPS, tiles, lats), lambda i: (0, 0, 0, 0)),
         ],
         out_specs=flux_spec,
         scratch_shapes=[mixed_shape],
         compiler_params=pltpu.CompilerParams(vmem_limit_bytes=VMEM_LIMIT),
-    )(flux_probes, time_pad.T, sel_t, back_lat)
+    )(flux_probes, time_pad.T, sel, back_lat)
 
 
 def solution(mesh):

time: 206 us -> 160 us (0.78)
  Pallas kernels: 174 us -> 137 us
  other arithmetic: 10.1 us -> 4.64 us
  local copies, waits for them, and re-layouts: 11 us -> 7.77 us
    pallas_call x1, Pallas kernels: 52.3 us -> 29.5 us  [reduce_blocks(): pl.pallas_call(functools.partial(reduce_kernel, n), out_shape=jax.ShapeDt...]
    pallas_call x1, Pallas kernels: 32.3 us -> 21.9 us  [body(): pl.pallas_call(forward_kernel, grid=(steps,), out_shape=jax.ShapeDtypeStr...]
    convert_element_type x1 -> x0, other arithmetic: 4.55 us -> none  [body(): jnp.where(slot[:, None, :] == row_slot[None, :, None], sel_t, 0.0)]
    dot_general x1 -> x0, local copies, waits for them, and re-layouts: 4.13 us -> none  [body(): sel_t = jnp.einsum('kr,gek->gre', lon_wide, hot, preferred_element_type=f32)]
    pallas_call x1, Pallas kernels: 32.6 us -> 28.9 us  [body(): pl.pallas_call(backward_kernel, grid=(steps,), out_shape=jax.ShapeDtypeSt...]
where the time goes in v2:
time: 160 us
  Pallas kernels  137 us (86%)
  matrix products  10.1 us (6%)
  local copies, waits for them, and re-layouts  7.77 us (5%)
  other arithmetic  4.64 us (3%)
    pallas_call x2, Pallas kernels, gather(): pl.pallas_call(functools.partial(gather_kernel, n), out_shape=jax.ShapeDt...  38.1 us
    pallas_call x1, Pallas kernels, reduce_blocks(): pl.pallas_call(functools.partial(reduce_kernel, n), out_shape=jax.ShapeDt...  29.5 us
    pallas_call x1, Pallas kernels, body(): pl.pallas_call(backward_kernel, grid=(steps,), out_shape=jax.ShapeDtypeSt...  28.9 us
    pallas_call x1, Pallas kernels, body(): pl.pallas_call(forward_kernel, grid=(steps,), out_shape=jax.ShapeDtypeStr...  21.9 us
    pallas_call x1, Pallas kernels, residuals(): pl.pallas_call(functools.partial(residual_kernel, n), out_shape=jax.Shape...  18.8 us
    dot_general x1, matrix products, body(): sel = jnp.einsum('gek,kr->ger', hot, lon_wide, preferred_element_type=f32)  4.02 us

profile of v2, /device:TPU:13, one launch (start us, length us, event | category | flops | bytes accessed | tf_op | source)
XLA Modules:
  0.0 159.7 jit_solution(9144700278321174455)
XLA Ops:
  0.0 0.0 copy-start
  0.0 0.8 bitcast_add_fusion
  0.8 1.3 pad.9.x_ref
  2.1 1.3 broadcast_bitcast_fusion.w_ref
  3.4 8.5 %shard_map.91 = s32[16,8,128]{2,1,0:T(8,128)} custom-call(s32[8,128]{1,0:T(8,128)} %pad.9.x_ref), custom_call_target="tpu_custom_call" | custom-call | tf_op jit(solution)/shard_map/pallas_call | solution.py:63
  11.9 0.8 slice.3
  12.8 0.1 add_select_fusion.3
  12.9 0.9 reshape.253
  13.8 0.0 copy-start.1
  13.8 0.8 copy.17
  14.6 1.7 %copy.18 = bf16[256,256]{0,1:T(8,128)(2,1)} copy(bf16[256,256]{1,0:T(8,128)(2,1)} %param.11) | data formatting | bytes 262144 | tf_op args[2]
  16.3 0.2 copy.19
  16.5 1.0 add_select_fusion.band_ref
  17.5 4.0 %select_convert_fusion.sel_ref = bf16[16,64,768]{2,1,0:T(8,128)(2,1)} fusion(s32[16,64]{1,0:T(8,128)S(1)} %get-tuple-element.10, s32[768]{0:T(1024)S(1)} %get-tuple-element.12, s32[16,64]{1,0:T(8,128)S(1)} %get-tuple-element.9, bf16[768,768]{1,0:T(8,128)(2,1)} %param.12, s32[]{:T(128)S(6)} %select_n.94, s32[768]{0:T(1024)S(1)} %get-tuple-element.11), kind=kOutput, calls=%fused_computation | convolution fusion | flops 1268355072 | bytes 1783812 | tf_op jit(solution)/shard_map/gek,kr->ger/dot_general | solution.py:286
  21.5 0.0 copy-done.1
  21.5 21.9 %shard_map.92.x_ref = bf16[16,64,512]{2,1,0:T(8,128)(2,1)} custom-call(bf16[48,4,192,256]{3,2,1,0:T(8,128)(2,1)} %flux_ref.3, bf16[256,192]{1,0:T(8,128)(2,1)} %bitcast.38, bf16[16,64,768]{2,1,0:T(8,128)(2,1)} %select_convert_fusion.sel_ref, bf16[256,256]{1,0:T(8,128)(2,1)} %bitcast.39, s32[16,64,1]{2,1,0:T(8,128)} %add_select_fusion.band_ref), custom_call_target="tpu_custom_call" | custom-call | tf_op jit(solution)/shard_map/pallas_call | solution.py:292
  43.5 29.5 %shard_map.93 = f32[64,512]{1,0:T(8,128)} custom-call(bf16[16,64,512]{2,1,0:T(8,128)(2,1)} %shard_map.92.x_ref), custom_call_target="tpu_custom_call" | custom-call | tf_op jit(solution)/shard_map/pallas_call | solution.py:115
  72.9 0.9 convert_element_type.37
  73.9 0.0 copy-done
  73.9 1.2 fusion.32
  75.1 0.1 reshape.261
  75.1 1.0 fusion.15.x_ref
  76.2 18.8 %shard_map.94 = f32[16,8,512]{2,1,0:T(8,128)} custom-call(f32[16,8,512]{2,1,0:T(8,128)} %fusion.15.x_ref, f32[8,512]{1,0:T(8,128)} %broadcast_bitcast_fusion.w_ref), custom_call_target="tpu_custom_call" | custom-call | tf_op jit(solution)/shard_map/pallas_call | solution.py:163
  94.9 1.2 convolution_convert_fusion.2
  96.1 0.7 convolution_convert_fusion.1
  96.8 0.6 copy.36
  97.4 0.0 copy-start.2
  97.4 29.6 %shard_map.95 = bf16[16,64,512]{2,1,0:T(8,128)(2,1)} custom-call(bf16[64,512]{1,0:T(8,128)(2,1)} %bitcast.42), custom_call_target="tpu_custom_call" | custom-call | tf_op jit(solution)/shard_map/pallas_call | solution.py:63
  127.0 1.8 %bitcast_select_fusion.1 = (bf16[16,64,4,128]{3,1,2,0:T(8,128)(2,1)S(1)}, bf16[16,64,4,128]{3,1,2,0:T(8,128)(2,1)S(1)}) fusion(pred[16,64]{1,0:T(8,128)(4,1)S(1)} %get-tuple-element.7, pred[16,64]{1,0:T(8,128)(4,1)S(1)} %get-tuple-element.8, bf16[16,64,512]{2,1,0:T(8,128)(2,1)} %shard_map.95), kind=kLoop, calls=%fused_computation.13 | loop fusion | flops 1048576 | bytes 3147776 | tf_op jit(solution)/shard_map/jit(_where)/select_n | solution.py:328
  128.8 0.0 copy-done.2
  128.8 2.1 %convert_bitcast_fusion.back_ref = bf16[4,16,64,256]{3,2,1,0:T(8,128)(2,1)} fusion(bf16[256,256]{1,0:T(8,128)(2,1)S(1)} %copy-done.2, bf16[16,64,4,128]{3,1,2,0:T(8,128)(2,1)S(1)} %get-tuple-element.6, bf16[16,64,4,128]{3,1,2,0:T(8,128)(2,1)S(1)} %get-tuple-element.5), kind=kOutput, calls=%fused_computation.6 | convolution fusion | flops 542113792 | bytes 4325376 | tf_op jit(solution)/shard_map/gepi,ij->pgej/dot_general | solution.py:330
  130.9 28.9 %shard_map.96 = bf16[48,4,192,256]{3,2,1,0:T(8,128)(2,1)} custom-call(bf16[48,4,192,256]{3,2,1,0:T(8,128)(2,1)} %flux_ref.3, bf16[192,256]{1,0:T(8,128)(2,1)} %bitcast.40, bf16[16,64,768]{2,1,0:T(8,128)(2,1)} %select_convert_fusion.sel_ref, bf16[4,16,64,256]{3,2,1,0:T(8,128)(2,1)} %convert_bitcast_fusion.back_ref), custom_call_target="tpu_custom_call" | custom-call | tf_op jit(solution)/shard_map/pallas_call | solution.py:334
  (7 shorter events, 0.1 us)
Async XLA Ops:
  0.0 73.9 %copy-start = (bf16[64,128,128]{2,1,0:T(8,128)(2,1)S(1)}, bf16[64,128,128]{2,1,0:T(8,128)(2,1)}, u32[]{:S(2)}) copy-start(bf16[64,128,128]{2,1,0:T(8,128)(2,1)} %param.13) | copy-start | bytes 6291460
  13.8 7.7 %copy-start.1 = (bf16[16,16,192]{2,1,0:T(8,128)(2,1)}, bf16[16,16,192]{2,1,0:T(8,128)(2,1)S(1)}, u32[]{:S(2)}) copy-start(bf16[16,16,192]{2,1,0:T(8,128)(2,1)S(1)} %pad.8) | copy-start | bytes 294916
  97.4 31.4 %copy-start.2 = (bf16[256,256]{1,0:T(8,128)(2,1)S(1)}, bf16[256,256]{1,0:T(8,128)(2,1)}, u32[]{:S(2)}) copy-start(bf16[256,256]{1,0:T(8,128)(2,1)} %param.11) | copy-start | bytes 393220
